TPU v7x, 256 devices: a whole 4x4x8 slice. The times are simulated.
256 devices in a mesh: replica: 16 (over x, z_hi), fsdp: 16 (over z_lo, y, core).
Axes of the slice: x: 4, y: 4, z: 8 (z_hi: 4, z_lo: 2; z = z_hi * 2 + z_lo), core: 2. Of those that a mesh axis runs over, the one named last changes fastest.
Arguments:
- base: bfloat16 [1024, 28672], P('fsdp')
- local: bfloat16 [16, 1024, 28672], P('replica', 'fsdp')
- momentum: float32 [1024, 28672], P('fsdp', 'replica'), may hold values from -0.6 to 0.6
Outputs:
- new_params: bfloat16 [1024, 28672], P('fsdp')
- new_momentum: float32 [1024, 28672], P('fsdp', 'replica')
- grad_rms: float32 [], replicated
All inputs are finite; a program needn't handle non-finite values.
Results may differ from a plain program's by a relative error of at most 0.008.
Values may be sent and summed in bfloat16 or wider, within the bound.
A program may use at most 128 MiB of HBM per device.

v0:
```python
import jax
import jax.numpy as jnp
from jax import lax
from jax.sharding import PartitionSpec as P

outer_rate = 0.7
momentum_decay = 0.9


def per_device(base, local, momentum):
    replicas = lax.axis_size("replica")
    base_wide = base.astype(jnp.float32)
    delta = base_wide - local[0].astype(jnp.float32)
    rows, columns = delta.shape
    blocks = delta.reshape(rows, columns // 128, 128)
    largest = jnp.max(jnp.abs(blocks), axis=2)
    scale_low = ((largest + 1e-06) / 448.0).astype(jnp.bfloat16)
    scale = lax.optimization_barrier(scale_low).astype(jnp.float32)
    coded = (blocks / scale[:, :, None]).astype(jnp.bfloat16)
    decoded_vals = (coded.astype(jnp.float32) * scale[:, :, None]).reshape(rows, columns)
    total = lax.psum_scatter(decoded_vals, "replica", scatter_dimension=1, tiled=True)
    outer_grad = total / replicas
    square_sum = lax.psum(jnp.sum(outer_grad * outer_grad), ("replica", "fsdp"))
    devices = replicas * lax.axis_size("fsdp")
    grad_rms = jnp.sqrt(square_sum / (outer_grad.size * devices))
    new_momentum = momentum_decay * momentum + outer_grad
    piece_cols = outer_grad.shape[1]
    owned_base = lax.dynamic_slice_in_dim(
        base_wide, lax.axis_index("replica") * piece_cols, piece_cols, 1
    )
    new_piece = (owned_base - outer_rate * (momentum_decay * new_momentum + outer_grad)).astype(
        jnp.bfloat16
    )
    new_params = lax.all_gather(new_piece, "replica", axis=1, tiled=True)
    return (new_params, new_momentum, grad_rms)


def solution(mesh):
    return jax.shard_map(
        per_device,
        mesh=mesh,
        in_specs=(P("fsdp", None), P("replica", "fsdp", None), P("fsdp", "replica")),
        out_specs=(P("fsdp", None), P("fsdp", "replica"), P()),
        check_vma=False,
    )
```

profile of v0, /device:TPU:1, one launch (start us, length us, event | category | flops | bytes accessed | tf_op | source)
XLA Modules:
  0.0 244.2 jit_solution(11838169495724962177)
XLA Ops:
  7.2 0.0 reduce-scatter.2.cloned.1.call-start
  7.2 4.1 %abs_bitcast_fusion = f32[8,8,224,128]{3,1,2,0:T(8,128)S(1)} fusion(bf16[1,64,28672]{2,1,0:T(8,128)(2,1)} %param.4, bf16[64,28672]{1,0:T(8,128)(2,1)} %param.3), kind=kLoop, calls=%fused_computation.4 | loop fusion | flops 7340032 | bytes 14680064
  11.4 4.3 %copy.6 = f32[8,8,224,128]{3,2,1,0:T(8,128)} copy(f32[8,8,224,128]{3,1,2,0:T(8,128)S(1)} %abs_bitcast_fusion) | data formatting | bytes 14680064
  15.6 5.3 %reduce_max.9 = f32[64,224]{1,0:T(8,128)S(1)} reduce(f32[64,224,128]{2,1,0:T(8,128)} %bitcast.15, f32[]{:T(128)} %constant.11.clone.1), dimensions={2}, to_apply=%region_0.0 | reduce | flops 1820672 | bytes 7397380 | tf_op jit(solution)/shard_map/reduce_max | solution.py:16
  21.0 0.0 copy-start
  21.0 0.0 copy-start.1
  21.0 2.0 div.28
  23.0 0.0 copy-done
  23.1 1.1 copy-done.1
  24.1 6.6 %bitcast_multiply_fusion = f32[64,28672]{1,0:T(8,128)} fusion(f32[8,8,224,128]{3,2,1,0:T(8,128)S(1)} %bitcast.16, bf16[1,64,28672]{2,1,0:T(8,128)(2,1)S(1)} %copy-done.1, bf16[64,28672]{1,0:T(8,128)(2,1)S(1)} %copy-done), kind=kLoop, calls=%fused_computation | loop fusion | flops 12845056 | bytes 22020096 | tf_op jit(solution)/shard_map/mul | solution.py:20
  30.7 0.0 reduce-scatter.2.cloned.1.call-update
  30.7 0.0 copy-start.2
  30.8 0.0 all-gather.2.cloned.1.call-start
  30.8 5.5 %convert_element_type.26 = f32[64,28672]{1,0:T(8,128)} convert(bf16[64,28672]{1,0:T(8,128)(2,1)} %param.3) | non-fusion elementwise | flops 1835008 | bytes 11010048 | tf_op jit(solution)/shard_map/convert_element_type | solution.py:12
  36.3 112.0 %reduce-scatter.2.cloned.1.call-done = f32[64,1792]{1,0:T(8,128)} async-done(((f32[64,28672]{1,0:T(8,128)}), f32[64,1792]{1,0:T(8,128)}) %reduce-scatter.2.cloned.1.call-update) | async-done | bytes 458768 | tf_op jit(solution)/shard_map/reduce_scatter | solution.py:21
  148.3 0.0 copy-done.2
  148.3 2.7 %subtract_convert_fusion = (bf16[64,1792]{1,0:T(8,128)(2,1)}, f32[64,1792]{1,0:T(8,128)}, f32[]{:T(128)}) fusion(f32[64,28672]{1,0:T(8,128)} %convert_element_type.26, s32[]{:T(128)S(6)} %select_n.3, f32[64,1792]{1,0:T(8,128)} %reduce-scatter.2.cloned.1.call-done, f32[64,1792]{1,0:T(8,128)S(1)} %copy-done.2), kind=kLoop, calls=%fused_computation.6 | loop fusion | flops 1146879 | bytes 2064392 | tf_op jit(solution)/shard_map/convert_element_type | solution.py:31
  151.1 0.0 all-gather.2.cloned.1.call-update
  151.1 80.3 %psum.7 = f32[]{:T(128)} all-reduce(f32[]{:T(128)} %get-tuple-element.5), channel_id=1, replica_groups=mesh['replica'=16,'fsdp'=16] {'replica','fsdp'}, use_global_device_ids=true, to_apply=%region_3.0 | all-reduce | flops 1 | bytes 8 | tf_op jit(solution)/shard_map/psum | solution.py:23
  232.1 0.0 all-gather.2.cloned.1.call-done
  232.1 4.1 %copy.13 = bf16[64,28672]{1,0:T(8,128)(2,1)} copy(bf16[64,28672]{1,0:T(8,128)(2,1)} %all-gather.2.cloned.1.call-done) | data formatting | bytes 7340032
  (1 shorter events, 0.0 us)
Async XLA Ops:
  7.2 141.2 %reduce-scatter.2.cloned.1.call-start = ((), (), s32[]{:S(2)}) async-start(), calls=%async_computation.1 | async-start | bytes 7798784 | tf_op jit(solution)/shard_map/reduce_scatter | solution.py:21
  21.0 2.1 copy-start
  21.0 3.2 %copy-start.1 = (bf16[1,64,28672]{2,1,0:T(8,128)(2,1)S(1)}, bf16[1,64,28672]{2,1,0:T(8,128)(2,1)}, u32[]{:S(2)}) copy-start(bf16[1,64,28672]{2,1,0:T(8,128)(2,1)} %param.4) | copy-start | bytes 11010052
  30.7 117.6 %copy-start.2 = (f32[64,1792]{1,0:T(8,128)S(1)}, f32[64,1792]{1,0:T(8,128)}, u32[]{:S(2)}) copy-start(f32[64,1792]{1,0:T(8,128)} %param.5) | copy-start | bytes 1376260
  30.8 201.4 %all-gather.2.cloned.1.call-start = ((), (), s32[]{:S(2)}) async-start(), calls=%async_computation.2 | async-start | bytes 3899392 | tf_op jit(solution)/shard_map/all_gather | solution.py:34
Sparse Core Ops, SparseCore 0:
  30.9 117.4 reduce-scatter.1
  151.7 73.0 all-gather.1
where the time goes:
time: 244 us
  waiting for transfers between devices  112 us (46%)
  blocking collectives  80.3 us (33%)
  other arithmetic  24.3 us (10%)
  between operations  15.9 us (7%)
  local copies, waits for them, and re-layouts  11.5 us (5%)
    reduce_scatter x1, waiting for transfers between devices, per_device(): lax.psum_scatter(decoded_vals, 'replica', scatter_dimension=1, tiled=True)  112 us
    psum x1, blocking collectives, per_device(): square_sum = lax.psum(jnp.sum(outer_grad * outer_grad), ('replica', 'fsdp'))  80.3 us
    unnamed x8, local copies, waits for them, and re-layouts  9.45 us
    mul x1, other arithmetic, per_device(): coded.astype(jnp.float32) * scale[:, :, None]  6.6 us
    convert_element_type x1, other arithmetic, per_device(): base_wide = base.astype(jnp.float32)  5.53 us
    reduce_max x1, other arithmetic, per_device(): largest = jnp.max(jnp.abs(blocks), axis=2)  5.31 us
  transfers between devices with their start and end apart: 2, of which 1 were waited for; matrix products, arithmetic and copies ran while one was open for 2% of the time, Pallas kernels for 0%

commit v1 on v0

v1 whole, which is shorter than its diff:
```python
import functools

import jax
import jax.numpy as jnp
from jax import lax
from jax.experimental import pallas as pl
from jax.experimental.pallas import tpu as pltpu
from jax.sharding import PartitionSpec as P

MESH = pl.DeviceIdType.MESH
LANES = 128
SIDE = 4
outer_rate = 0.7
momentum_decay = 0.9

CHUNKS = ((0, 4, "x"), (11, 3, "z"), (4, 4, "x"), (8, 3, "x"))
ORDER = (
    ("e0", 0), ("e0", 1), ("e1", 0), ("e1", 1), ("e2", 0), ("e3", 0), ("e0", 2), ("e1", 2), ("e2", 1), ("e3", 1),
    ("r3", 0), ("e0", 3), ("e1", 3), ("e2", 2), ("e3", 2), ("e3", 3), ("r4", 0), ("r5", 0),
    ("r3", 1), ("r3", 2), ("e2", 3), ("r4", 1), ("g6", 0), ("r4", 2), ("r5", 1), ("g7", 0), ("r5", 2),
    ("r3", 3), ("g6", 1), ("r4", 3), ("g6", 2), ("g7", 1), ("r5", 3), ("n0", 0), ("g7", 2), ("g8", 0), ("g6", 3),
    ("n1", 0), ("g8", 1), ("g7", 3), ("n2", 0), ("g8", 2), ("n3", 0), ("g8", 3), ("g9", 0), ("g9", 1), ("g9", 2), ("g9", 3),
)


def kernel(
    base_hbm, local_hbm, momentum_hbm, params_ref, new_momentum_ref, rms_ref,
    base_ref, local_ref, momentum_ref, coded_ref,
    full_l, full_r, half_l, half_r, last_l, last_r, part_l, part_r,
    squares_ref, norm_ref, load_sem, send_sem, recv_sem,
):
    rows, columns = base_ref.shape
    half = rows // 2
    piece = columns // (SIDE * SIDE)
    replica = lax.axis_index("replica")
    fsdp = lax.axis_index("fsdp")
    at = {"x": replica // SIDE, "z": replica % SIDE}
    near, z_lo = fsdp % 2, fsdp // 8
    y = (fsdp // 2) % 4

    def shifted(axis, step):
        return (at[axis] + step + SIDE) % SIDE

    def device(axis, step):
        x, z = at["x"], at["z"]
        if axis == "x":
            x = shifted("x", step)
        else:
            z = shifted("z", step)
        return (x * SIDE + z, fsdp)

    def fsdp_device(axis, step):
        if axis == "y":
            return (replica, z_lo * 8 + (y + step) % 4 * 2 + near)
        other = (z_lo * 2 + near + step) % 4
        return (replica, other // 2 * 8 + y * 2 + other % 2)

    group = SIDE * piece
    loads = {}
    for i, step in enumerate((2, 1, -1, 0)):
        cols = pl.ds(pl.multiple_of(shifted("x", step) * group, LANES), group)
        loads[step] = (
            pltpu.make_async_copy(base_hbm.at[:, cols], base_ref.at[:, cols], load_sem.at[2 * i]),
            pltpu.make_async_copy(local_hbm.at[0, :, cols], local_ref.at[:, cols], load_sem.at[2 * i + 1]),
        )
        for copy in loads[step]:
            copy.start()
    momentum_load = pltpu.make_async_copy(momentum_hbm, momentum_ref, load_sem.at[8])
    momentum_load.start()
    squares_ref[...] = jnp.zeros_like(squares_ref)

    barrier = pltpu.get_barrier_semaphore()
    peers = [device(axis, step) for axis in ("x", "z") for step in (1, 2, 3)]
    peers += [fsdp_device(axis, step) for axis in ("y", "other") for step in (1, 2, 3)]
    for peer in peers:
        pl.semaphore_signal(barrier, inc=1, device_id=peer, device_id_type=MESH)
    entered = []
    waited = set()

    def loaded(step):
        if step not in waited:
            waited.add(step)
            for copy in loads[step]:
                copy.wait()

    copies = {}

    def send(key, src, dst, target):
        if not entered:
            entered.append(True)
            pl.semaphore_wait(barrier, len(peers))
        i = len(copies)
        copy = pltpu.make_async_remote_copy(
            src_ref=src, dst_ref=dst, send_sem=send_sem.at[i], recv_sem=recv_sem.at[i],
            device_id=target, device_id_type=MESH,
        )
        copy.start()
        copies[key] = copy

    def recv(*key):
        copies[key].wait_recv()

    low, high, every = pl.ds(0, half), pl.ds(half, half), pl.ds(0, rows)

    def column(x, z, block):
        return pl.multiple_of((x * SIDE + z) * piece + block * LANES, LANES)

    def code_block(block, x, z):
        cols = pl.ds(column(x, z, block), LANES)
        delta = base_ref[:, cols].astype(jnp.float32) - local_ref[:, cols].astype(jnp.float32)
        largest = jnp.max(jnp.abs(delta), axis=1, keepdims=True)
        scale = ((largest + 1e-06) * (1.0 / 448.0)).astype(jnp.bfloat16).astype(jnp.float32)
        coded = (delta / scale).astype(jnp.bfloat16).astype(jnp.float32)
        coded_ref[block, x, z] = (coded * scale).astype(jnp.bfloat16)

    def over(start, count, body, unroll=2):
        def step(i, carry):
            body(start + i // SIDE, i % SIDE)
            return carry
        lax.fori_loop(0, count * SIDE, step, 0, unroll=unroll)

    def blocks(start, count, body):
        def step(i, carry):
            body(start + i)
            return carry
        lax.fori_loop(0, count, step, 0)

    def f32(value):
        return value.astype(jnp.float32)

    steps = {}
    for c, (start, count, first) in enumerate(CHUNKS):
        second = "z" if first == "x" else "x"
        ks = pl.ds(start, count)

        def xz(f, s, first=first):
            return (f, s) if first == "x" else (s, f)

        def row_of(f, rs, ks=ks, first=first):
            if first == "x":
                return coded_ref.at[ks, f, :, rs]
            return coded_ref.at[ks, :, f, rs]

        def piece_of(f, s, rs, ks=ks, xz=xz):
            return coded_ref.at[(ks, *xz(f, s), rs)]

        def gathered(f, s, rs, start=start, count=count, xz=xz):
            return params_ref.at[rs, pl.ds(column(*xz(f, s), start), count * LANES)]

        def code(f_step, start=start, count=count, first=first, xz=xz):
            if first == "x":
                loaded(f_step)
            else:
                for step in (2, 1, -1, 0):
                    loaded(step)
            f = shifted(first, f_step)
            over(start, count, lambda block, s: code_block(block, *xz(f, s)))

        def e0(c=c, ks=ks, first=first, row_of=row_of, code=code):
            code(2)
            far = shifted(first, 2)
            send(("p_r", c), row_of(far, low), half_l.at[ks], device(first, 1))
            send(("p_l", c), row_of(far, high), half_r.at[ks], device(first, -1))

        def e1(c=c, ks=ks, first=first, row_of=row_of, code=code):
            code(1)
            send(("w_r", c), row_of(shifted(first, 1), high), full_l.at[ks, :, high], device(first, 1))
            code(-1)
            send(("w_l", c), row_of(shifted(first, -1), low), full_r.at[ks, :, low], device(first, -1))

        def e2(c=c, ks=ks, start=start, count=count, first=first, row_of=row_of, xz=xz):
            for name, step, rs, got, into in (
                ("r", 1, low, half_l, full_l), ("l", -1, high, half_r, full_r),
            ):
                f = shifted(first, step)
                recv("p_" + name, c)

                def add(block, s, f=f, rs=rs, got=got):
                    index = (block, *xz(f, s), rs)
                    coded_ref[index] = (f32(coded_ref[index]) + f32(got[block, s])).astype(jnp.bfloat16)
                over(start, count, add)
                send(("s_" + name, c), row_of(f, rs), into.at[ks, :, rs], device(first, step))

        def e3(code=code):
            code(0)

        def r3(c=c, ks=ks, start=start, count=count, first=first, second=second, piece_of=piece_of, xz=xz):
            for name in ("w_r", "w_l", "s_r", "s_l"):
                recv(name, c)
            f = at[first]

            def add(block, s):
                index = (block, *xz(f, s))
                total = f32(coded_ref[index]) + f32(full_l[block, s]) + f32(full_r[block, s])
                coded_ref[index] = total.astype(jnp.bfloat16)
            over(start, count, add)
            far = shifted(second, 2)
            send(("P_r", c), piece_of(f, far, low), part_l.at[ks], device(second, 1))
            send(("P_l", c), piece_of(f, far, high), part_r.at[ks], device(second, -1))
            send(("W_r", c), piece_of(f, shifted(second, 1), high), last_l.at[ks, high], device(second, 1))
            send(("W_l", c), piece_of(f, shifted(second, -1), low), last_r.at[ks, low], device(second, -1))

        def r4(c=c, ks=ks, start=start, count=count, first=first, second=second, piece_of=piece_of, xz=xz):
            f = at[first]
            for name, step, rs, got, into in (
                ("r", 1, low, part_l, last_l), ("l", -1, high, part_r, last_r),
            ):
                s = shifted(second, step)
                recv("P_" + name, c)

                def add(block, s=s, rs=rs, got=got):
                    index = (block, *xz(f, s), rs)
                    coded_ref[index] = (f32(coded_ref[index]) + f32(got[block])).astype(jnp.bfloat16)
                blocks(start, count, add)
                send(("S_" + name, c), piece_of(f, s, rs), into.at[ks, rs], device(second, step))

        def spread(c, first, gathered, s):
            for name, step in (("r", 1), ("l", -1)):
                part = gathered(at[first], shifted(second_of[first], s), every)
                send(("G_" + name, s, c), part, part, device(first, step))

        def r5(c=c, start=start, count=count, first=first, second=second, gathered=gathered, spread=spread):
            for name in ("W_r", "W_l", "S_r", "S_l"):
                recv(name, c)
            if "momentum" not in waited:
                waited.add("momentum")
                momentum_load.wait()

            def update(block):
                x, z = at["x"], at["z"]
                total = f32(coded_ref[block, x, z]) + f32(last_l[block]) + f32(last_r[block])
                grad = total * (1.0 / (SIDE * SIDE))
                squares_ref[...] += jnp.sum((grad * grad).reshape(rows // 8, 8, LANES), axis=0)
                own = pl.ds(pl.multiple_of(block * LANES, LANES), LANES)
                new_momentum = momentum_decay * momentum_ref[:, own] + grad
                new_momentum_ref[:, own] = new_momentum
                cols = pl.ds(column(x, z, block), LANES)
                stepped = f32(base_ref[:, cols]) - outer_rate * (momentum_decay * new_momentum + grad)
                params_ref[:, cols] = stepped.astype(jnp.bfloat16)
            blocks(start, count, update)
            mine = gathered(at[first], at[second], every)
            send(("g_r", c), mine, mine, device(second, 1))
            send(("g_l", c), mine, mine, device(second, -1))
            spread(c, first, gathered, 0)

        def g6(c=c, first=first, second=second, gathered=gathered, spread=spread):
            for name, step, rs in (("r", 1, low), ("l", -1, high)):
                recv("g_" + name, c)
                passed = gathered(at[first], shifted(second, -step), rs)
                send(("h_" + name, c), passed, passed, device(second, step))
            spread(c, first, gathered, 1)
            spread(c, first, gathered, -1)

        def g7(c=c, first=first, gathered=gathered, spread=spread):
            recv("h_r", c)
            recv("h_l", c)
            spread(c, first, gathered, 2)

        def g8(c=c, first=first, second=second, gathered=gathered):
            for s in (0, 1, -1, 2):
                for name, step, rs in (("r", 1, low), ("l", -1, high)):
                    recv("G_" + name, s, c)
                    passed = gathered(shifted(first, -step), shifted(second, s), rs)
                    send(("H_" + name, s, c), passed, passed, device(first, step))

        def g9(c=c):
            for s in (0, 1, -1, 2):
                recv("H_r", s, c)
                recv("H_l", s, c)

        for step in (e0, e1, e2, e3, r3, r4, r5, g6, g7, g8, g9):
            steps[step.__name__, c] = step

    def norm_round(i, place, target):
        for step in (1, 2, 3):
            send(("n", i, step), norm_ref.at[i, place], norm_ref.at[i, place], target(step))

    def norm_sum(i):
        for step in (1, 2, 3):
            recv("n", i, step)
        return norm_ref[i, 0] + norm_ref[i, 1] + norm_ref[i, 2] + norm_ref[i, 3]

    other = z_lo * 2 + near

    def n0():
        norm_ref[0, at["x"]] = squares_ref[...]
        norm_round(0, at["x"], lambda step: device("x", step))

    def n1():
        norm_ref[1, at["z"]] = norm_sum(0)
        norm_round(1, at["z"], lambda step: device("z", step))

    def n2():
        norm_ref[2, y] = norm_sum(1)
        norm_round(2, y, lambda step: fsdp_device("y", step))

    def n3():
        norm_ref[3, other] = norm_sum(2)
        norm_round(3, other, lambda step: fsdp_device("other", step))

    for step in (n0, n1, n2, n3):
        steps[step.__name__, 0] = step

    for key in ORDER:
        steps[key]()
    total = jnp.sum(norm_sum(3), axis=(0, 1), keepdims=True)
    entries = rows * columns * 16
    rms_ref[...] = jnp.broadcast_to(jnp.sqrt(total / entries), rms_ref.shape)
    for copy in copies.values():
        copy.wait_send()


second_of = {"x": "z", "z": "x"}
COPIES = len(CHUNKS) * (4 + 2 + 2 + 4 + 8 + 8 + 4) + 12


def per_device(base, local, momentum):
    rows, columns = base.shape
    piece = columns // (SIDE * SIDE)
    number = piece // LANES
    half = rows // 2
    bf16 = functools.partial(pltpu.VMEM, dtype=jnp.bfloat16)
    vmem = pl.BlockSpec(memory_space=pltpu.VMEM)
    new_params, new_momentum, rms = pl.pallas_call(
        kernel,
        out_shape=(
            pltpu.VMEM((rows, columns), jnp.bfloat16),
            pltpu.VMEM((rows, piece), jnp.float32),
            pltpu.VMEM((8, LANES), jnp.float32),
        ),
        in_specs=[pl.BlockSpec(memory_space=pltpu.HBM)] * 3,
        out_specs=(vmem, vmem, vmem),
        scratch_shapes=[
            bf16((rows, columns)),
            bf16((rows, columns)),
            pltpu.VMEM((rows, piece), jnp.float32),
            bf16((number, SIDE, SIDE, rows, LANES)),
            bf16((number, SIDE, rows, LANES)),
            bf16((number, SIDE, rows, LANES)),
            bf16((number, SIDE, half, LANES)),
            bf16((number, SIDE, half, LANES)),
            bf16((number, rows, LANES)),
            bf16((number, rows, LANES)),
            bf16((number, half, LANES)),
            bf16((number, half, LANES)),
            pltpu.VMEM((8, LANES), jnp.float32),
            pltpu.VMEM((4, 4, 8, LANES), jnp.float32),
            pltpu.SemaphoreType.DMA((9,)),
            pltpu.SemaphoreType.DMA((COPIES,)),
            pltpu.SemaphoreType.DMA((COPIES,)),
        ],
        compiler_params=pltpu.CompilerParams(
            collective_id=0, has_side_effects=True, vmem_limit_bytes=40 * 2**20
        ),
        name="outer_step",
    )(*(pltpu.with_memory_space_constraint(a, pltpu.HBM) for a in (base, local, momentum)))
    return (new_params, new_momentum, rms[0, 0])


def solution(mesh):
    return jax.shard_map(
        per_device,
        mesh=mesh,
        in_specs=(P("fsdp", None), P("replica", "fsdp", None), P("fsdp", "replica")),
        out_specs=(P("fsdp", None), P("fsdp", "replica"), P()),
        check_vma=False,
    )
```

time: 244 us -> 83.7 us (0.34)
  waiting for transfers between devices: 112 us -> 0 us
  blocking collectives: 80.3 us -> 0 us
  Pallas kernels: 0 us -> 79.2 us
  other arithmetic: 24.3 us -> 0 us
  between operations: 15.9 us -> 0.64 us
  local copies, waits for them, and re-layouts: 11.5 us -> 3.12 us
    reduce_scatter x1 -> x0, waiting for transfers between devices: 112 us -> none  [per_device(): lax.psum_scatter(decoded_vals, 'replica', scatter_dimension=1, tiled=True)]
    psum x1 -> x0, blocking collectives: 80.3 us -> none  [per_device(): square_sum = lax.psum(jnp.sum(outer_grad * outer_grad), ('replica', 'fsdp'))]
    pallas_call x0 -> x1, Pallas kernels: none -> 79.2 us  [per_device(): pl.pallas_call(kernel, out_shape=(pltpu.VMEM((rows, columns), jnp.bfloat1...]
    convert_element_type x3 -> x0, other arithmetic: 8.28 us -> none  [the longest x1 5.53 us: per_device(): base_wide = base.astype(jnp.float32)]
    unnamed x8 -> x2, local copies, waits for them, and re-layouts: 9.45 us -> 2.6 us
    mul x1 -> x0, other arithmetic: 6.6 us -> none  [per_device(): coded.astype(jnp.float32) * scale[:, :, None]]
    reduce_max x1 -> x0, other arithmetic: 5.31 us -> none  [per_device(): largest = jnp.max(jnp.abs(blocks), axis=2)]
    unnamed x1 -> x0, other arithmetic: 4.14 us -> none
  transfers between devices with their start and end apart: 2 -> 0, of which waited for: 1 -> 0; matrix products, arithmetic and copies ran while one was open for 2% -> 0% of each run, Pallas kernels for 0% -> 0%
where the time goes in v1:
time: 83.7 us; the launch traced here: 82.9 us
  Pallas kernels  79.2 us (95%)
  local copies, waits for them, and re-layouts  3.12 us (4%)
    pallas_call x1, Pallas kernels, per_device(): pl.pallas_call(kernel, out_shape=(pltpu.VMEM((rows, columns), jnp.bfloat1...  79.2 us
    unnamed x2, local copies, waits for them, and re-layouts  2.6 us

profile of v1, /device:TPU:1, one launch (start us, length us, event | category | flops | bytes accessed | tf_op | source)
XLA Modules:
  0.0 82.9 jit_solution(16033472572175833558)
XLA Ops:
  0.6 79.2 %outer_step.1 = (bf16[64,28672]{1,0:T(8,128)(2,1)S(1)}, f32[64,1792]{1,0:T(8,128)S(1)}, f32[8,128]{1,0:T(8,128)S(1)}) custom-call(bf16[64,28672]{1,0:T(8,128)(2,1)} %base_hbm.1, bf16[1,64,28672]{2,1,0:T(8,128)(2,1)} %local_hbm.1, f32[64,1792]{1,0:T(8,128)} %momentum_hbm.1), custom_call_target="tpu_custom_call" | custom-call | tf_op jit(solution)/shard_map/outer_step/pallas_call | solution.py:324
  79.8 0.5 slice.3
  80.3 1.8 %copy.8 = bf16[64,28672]{1,0:T(8,128)(2,1)} copy(bf16[64,28672]{1,0:T(8,128)(2,1)S(1)} %get-tuple-element.9) | data formatting | bytes 7340032
  82.2 0.8 copy.9

commit v2 on v1

--- a/solution.py
+++ b/solution.py
@@ -13,13 +13,41 @@
 outer_rate = 0.7
 momentum_decay = 0.9
 
-CHUNKS = ((0, 4, "x"), (11, 3, "z"), (4, 4, "x"), (8, 3, "x"))
+CHUNKS = (
+    (0, 2, "x"),
+    (11, 1, "z"),
+    (2, 2, "x"),
+    (12, 1, "z"),
+    (4, 2, "x"),
+    (13, 1, "z"),
+    (6, 2, "x"),
+    (8, 2, "x"),
+    (10, 1, "x"),
+)
 ORDER = (
-    ("e0", 0), ("e0", 1), ("e1", 0), ("e1", 1), ("e2", 0), ("e3", 0), ("e0", 2), ("e1", 2), ("e2", 1), ("e3", 1),
-    ("r3", 0), ("e0", 3), ("e1", 3), ("e2", 2), ("e3", 2), ("e3", 3), ("r4", 0), ("r5", 0),
-    ("r3", 1), ("r3", 2), ("e2", 3), ("r4", 1), ("g6", 0), ("r4", 2), ("r5", 1), ("g7", 0), ("r5", 2),
-    ("r3", 3), ("g6", 1), ("r4", 3), ("g6", 2), ("g7", 1), ("r5", 3), ("n0", 0), ("g7", 2), ("g8", 0), ("g6", 3),
-    ("n1", 0), ("g8", 1), ("g7", 3), ("n2", 0), ("g8", 2), ("n3", 0), ("g8", 3), ("g9", 0), ("g9", 1), ("g9", 2), ("g9", 3),
+    ("E2", 2), ("Sp", 2), ("E2", 5), ("E2", 1), ("Sp", 5), ("E2", 0), ("Sp", 0), ("Sp", 1), ("E1l", 2), ("E1r", 0), ("Swr", 0), ("Swl", 2), ("E2", 3),
+    ("E1l", 5), ("E1l", 0), ("E1r", 2), ("Swl", 5), ("Swl", 0), ("Sp", 3), ("Swr", 2), ("A2r", 2), ("E1r", 5), ("E1l", 1), ("E1l", 8), ("A2l", 2),
+    ("A2r", 0), ("Swr", 5), ("E1r", 1), ("A2l", 0), ("Swl", 8), ("A2r", 5), ("A2l", 5), ("E2", 7), ("A2l", 1), ("E2", 4), ("E2", 8), ("Sp", 8),
+    ("E1r", 8), ("A2r", 1), ("Sp", 4), ("E1l", 4), ("E2", 6), ("Swr", 8), ("E0", 2), ("R3a", 2), ("E1l", 3), ("Swl", 1), ("Sp", 6), ("Swr", 1),
+    ("E0", 3), ("E0", 0), ("E1l", 6), ("Sp", 7), ("R3a", 0), ("E1r", 4), ("A2r", 8), ("R3b", 2), ("A2l", 8), ("E0", 5), ("R3b", 0), ("Swl", 4),
+    ("R3c", 2), ("Swr", 4), ("E1r", 6), ("R4r", 2), ("R4l", 2), ("A2l", 4), ("A2l", 3), ("E1r", 3), ("Swr", 3), ("E1r", 7), ("Swl", 6), ("A2r", 4),
+    ("E0", 4), ("A2l", 6), ("R4r", 0), ("R4l", 0), ("Swr", 6), ("Swl", 3), ("A2r", 6), ("A2r", 3), ("A2r", 7), ("Swr", 7), ("E1l", 7), ("E0", 8),
+    ("R3a", 8), ("Swl", 7), ("R3b", 8), ("R3c", 0), ("A2l", 7), ("R5", 2), ("R3a", 5), ("E0", 6), ("R3a", 4), ("R5", 0), ("R3b", 4), ("R3a", 3),
+    ("E0", 7), ("R3c", 3), ("R3a", 6), ("R4l", 8), ("R3c", 4), ("R4r", 8), ("R3c", 8), ("E0", 1), ("G6r", 2), ("G6l", 2), ("R3b", 6), ("R4l", 4),
+    ("R4r", 4), ("R3a", 7), ("R3a", 1), ("R3b", 5), ("R4r", 5), ("R4l", 5), ("G6l", 0), ("G6r", 0), ("R3c", 6), ("R3c", 5), ("R4r", 6), ("R4l", 6),
+    ("R3b", 3), ("R5", 8), ("R3b", 7), ("G8l", 2, 0), ("R3c", 7), ("R4r", 3), ("R3b", 1), ("G8l", 2, -1), ("R5", 5), ("G7", 2), ("R4r", 7),
+    ("R4l", 7), ("R4l", 3), ("R4l", 1), ("G8r", 2, 1), ("R4r", 1), ("G8l", 0, 1), ("R5", 4), ("G8r", 0, 0), ("G6r", 8), ("R3c", 1), ("G6l", 8),
+    ("R5", 6), ("R5", 3), ("G7", 0), ("R5", 7), ("R5", 1), ("N0", 0), ("G8r", 0, -1), ("G8l", 0, 0), ("G8l", 4, 0), ("G8r", 0, 1), ("G6l", 4),
+    ("G6r", 4), ("G8r", 8, 1), ("G8l", 2, 1), ("G6l", 3), ("G6r", 3), ("G8l", 0, -1), ("G6r", 6), ("G7", 8), ("G8l", 0, 2), ("G8r", 2, 0), ("G6r", 1),
+    ("G6l", 1), ("G6r", 7), ("G8r", 2, -1), ("G8r", 6, 0), ("G6r", 5), ("G6l", 7), ("G8r", 4, -1), ("G8r", 8, -1), ("G6l", 5), ("N1", 0), ("G7", 4),
+    ("G6l", 6), ("G8l", 2, 2), ("G8l", 4, -1), ("G8r", 4, 0), ("G8l", 3, 0), ("G7", 1), ("G8r", 7, 0), ("G7", 3), ("G8r", 4, 1), ("G8l", 6, 0),
+    ("G8l", 6, -1), ("G8r", 0, 2), ("G8r", 8, 2), ("G8l", 4, 1), ("G7", 5), ("G8l", 7, 0), ("G8r", 3, 0), ("G8l", 3, -1), ("G7", 7), ("G8r", 3, -1),
+    ("G8l", 5, -1), ("N2", 0), ("G8l", 8, 1), ("G8l", 1, -1), ("G8r", 3, 1), ("G8l", 8, 0), ("G8r", 5, -1), ("G8l", 1, 1), ("G8r", 6, -1), ("G7", 6),
+    ("G8r", 1, 0), ("G8l", 8, 2), ("G8r", 7, 1), ("G8r", 1, -1), ("G8r", 5, 0), ("G8l", 5, 1), ("G8l", 3, 1), ("G8r", 4, 2), ("G8r", 1, 2),
+    ("G8l", 7, -1), ("G8r", 1, 1), ("G8r", 7, -1), ("G8r", 2, 2), ("N3", 0), ("G8r", 3, 2), ("G8l", 1, 0), ("G8l", 4, 2), ("G8l", 6, 1),
+    ("G8l", 1, 2), ("G8l", 3, 2), ("G8r", 6, 1), ("G8r", 5, 2), ("G8r", 8, 0), ("G8l", 8, -1), ("G8r", 7, 2), ("G8l", 7, 2), ("G8r", 5, 1),
+    ("G8l", 5, 2), ("G8l", 5, 0), ("G8l", 7, 1), ("G8r", 6, 2), ("G8l", 6, 2), ("G9", 0), ("G9", 2), ("G9", 4), ("G9", 8), ("G9", 1), ("G9", 7),
+    ("G9", 3), ("G9", 6), ("G9", 5),
 )
 
 
@@ -83,22 +111,27 @@
             for copy in loads[step]:
                 copy.wait()
 
-    copies = {}
+    groups = {}
 
     def send(key, src, dst, target):
         if not entered:
             entered.append(True)
             pl.semaphore_wait(barrier, len(peers))
-        i = len(copies)
-        copy = pltpu.make_async_remote_copy(
-            src_ref=src, dst_ref=dst, send_sem=send_sem.at[i], recv_sem=recv_sem.at[i],
+        together = (GROUP[key[0]], key[-1]) if key[0] in GROUP else key
+        i = groups.setdefault(together, len(groups))
+        pltpu.make_async_remote_copy(
+            src_ref=src, dst_ref=dst, send_sem=send_sem.at[key[-1]], recv_sem=recv_sem.at[i],
             device_id=target, device_id_type=MESH,
-        )
-        copy.start()
-        copies[key] = copy
-
-    def recv(*key):
-        copies[key].wait_recv()
+        ).start()
+
+    def wait(sem, sized):
+        pltpu.make_async_copy(sized, sized, sem).wait()
+
+    def recv(key, sized):
+        wait(recv_sem.at[groups[key]], sized)
+
+    def pieces(count, x, z, rs=slice(None)):
+        return coded_ref.at[pl.ds(0, count), pl.ds(0, x), pl.ds(0, z), rs]
 
     low, high, every = pl.ds(0, half), pl.ds(half, half), pl.ds(0, rows)
 
@@ -156,72 +189,93 @@
             f = shifted(first, f_step)
             over(start, count, lambda block, s: code_block(block, *xz(f, s)))
 
-        def e0(c=c, ks=ks, first=first, row_of=row_of, code=code):
+
+        def E2(code=code):
             code(2)
+
+        def E1r(code=code):
+            code(1)
+
+        def E1l(code=code):
+            code(-1)
+
+        def E0(code=code):
+            code(0)
+
+        def Sp(c=c, ks=ks, first=first, row_of=row_of):
             far = shifted(first, 2)
             send(("p_r", c), row_of(far, low), half_l.at[ks], device(first, 1))
             send(("p_l", c), row_of(far, high), half_r.at[ks], device(first, -1))
 
-        def e1(c=c, ks=ks, first=first, row_of=row_of, code=code):
-            code(1)
+        def Swr(c=c, ks=ks, first=first, row_of=row_of):
             send(("w_r", c), row_of(shifted(first, 1), high), full_l.at[ks, :, high], device(first, 1))
-            code(-1)
+
+        def Swl(c=c, ks=ks, first=first, row_of=row_of):
             send(("w_l", c), row_of(shifted(first, -1), low), full_r.at[ks, :, low], device(first, -1))
 
-        def e2(c=c, ks=ks, start=start, count=count, first=first, row_of=row_of, xz=xz):
-            for name, step, rs, got, into in (
-                ("r", 1, low, half_l, full_l), ("l", -1, high, half_r, full_r),
-            ):
-                f = shifted(first, step)
-                recv("p_" + name, c)
-
-                def add(block, s, f=f, rs=rs, got=got):
-                    index = (block, *xz(f, s), rs)
-                    coded_ref[index] = (f32(coded_ref[index]) + f32(got[block, s])).astype(jnp.bfloat16)
-                over(start, count, add)
-                send(("s_" + name, c), row_of(f, rs), into.at[ks, :, rs], device(first, step))
-
-        def e3(code=code):
-            code(0)
-
-        def r3(c=c, ks=ks, start=start, count=count, first=first, second=second, piece_of=piece_of, xz=xz):
-            for name in ("w_r", "w_l", "s_r", "s_l"):
-                recv(name, c)
-            f = at[first]
+        def join(name, step, rs, got, into, c=c, ks=ks, start=start, count=count, first=first, row_of=row_of, xz=xz):
+            f = shifted(first, step)
+            recv(("p_" + name, c), pieces(count, 4, 1, low))
 
             def add(block, s):
-                index = (block, *xz(f, s))
+                index = (block, *xz(f, s), rs)
+                coded_ref[index] = (f32(coded_ref[index]) + f32(got[block, s])).astype(jnp.bfloat16)
+            over(start, count, add)
+            send(("s_" + name, c), row_of(f, rs), into.at[ks, :, rs], device(first, step))
+
+        def A2r(join=join):
+            join("r", 1, low, half_l, full_l)
+
+        def A2l(join=join):
+            join("l", -1, high, half_r, full_r)
+
+        def total_at(s, start=start, count=count, first=first, xz=xz):
+            def add(block):
+                index = (block, *xz(at[first], s))
                 total = f32(coded_ref[index]) + f32(full_l[block, s]) + f32(full_r[block, s])
                 coded_ref[index] = total.astype(jnp.bfloat16)
-            over(start, count, add)
+            blocks(start, count, add)
+
+        def R3a(c=c, ks=ks, count=count, first=first, second=second, piece_of=piece_of, total_at=total_at):
+            recv(("first", c), pieces(count, 4, 2))
             far = shifted(second, 2)
-            send(("P_r", c), piece_of(f, far, low), part_l.at[ks], device(second, 1))
-            send(("P_l", c), piece_of(f, far, high), part_r.at[ks], device(second, -1))
-            send(("W_r", c), piece_of(f, shifted(second, 1), high), last_l.at[ks, high], device(second, 1))
-            send(("W_l", c), piece_of(f, shifted(second, -1), low), last_r.at[ks, low], device(second, -1))
-
-        def r4(c=c, ks=ks, start=start, count=count, first=first, second=second, piece_of=piece_of, xz=xz):
-            f = at[first]
-            for name, step, rs, got, into in (
-                ("r", 1, low, part_l, last_l), ("l", -1, high, part_r, last_r),
-            ):
+            total_at(far)
+            send(("P_r", c), piece_of(at[first], far, low), part_l.at[ks], device(second, 1))
+            send(("P_l", c), piece_of(at[first], far, high), part_r.at[ks], device(second, -1))
+
+        def R3b(c=c, ks=ks, first=first, second=second, piece_of=piece_of, total_at=total_at):
+            for name, step, rs, into in (("r", 1, high, last_l), ("l", -1, low, last_r)):
                 s = shifted(second, step)
-                recv("P_" + name, c)
-
-                def add(block, s=s, rs=rs, got=got):
-                    index = (block, *xz(f, s), rs)
-                    coded_ref[index] = (f32(coded_ref[index]) + f32(got[block])).astype(jnp.bfloat16)
-                blocks(start, count, add)
-                send(("S_" + name, c), piece_of(f, s, rs), into.at[ks, rs], device(second, step))
-
-        def spread(c, first, gathered, s):
+                total_at(s)
+                send(("W_" + name, c), piece_of(at[first], s, rs), into.at[ks, rs], device(second, step))
+
+        def R3c(second=second, total_at=total_at):
+            total_at(at[second])
+
+        def last_join(name, step, rs, got, into, c=c, ks=ks, start=start, count=count, first=first, second=second,
+                      piece_of=piece_of, xz=xz):
+            s = shifted(second, step)
+            recv(("P_" + name, c), pieces(count, 1, 1, low))
+
+            def add(block):
+                index = (block, *xz(at[first], s), rs)
+                coded_ref[index] = (f32(coded_ref[index]) + f32(got[block])).astype(jnp.bfloat16)
+            blocks(start, count, add)
+            send(("S_" + name, c), piece_of(at[first], s, rs), into.at[ks, rs], device(second, step))
+
+        def R4r(last_join=last_join):
+            last_join("r", 1, low, part_l, last_l)
+
+        def R4l(last_join=last_join):
+            last_join("l", -1, high, part_r, last_r)
+
+        def spread(s, c=c, first=first, second=second, gathered=gathered):
             for name, step in (("r", 1), ("l", -1)):
-                part = gathered(at[first], shifted(second_of[first], s), every)
+                part = gathered(at[first], shifted(second, s), every)
                 send(("G_" + name, s, c), part, part, device(first, step))
 
-        def r5(c=c, start=start, count=count, first=first, second=second, gathered=gathered, spread=spread):
-            for name in ("W_r", "W_l", "S_r", "S_l"):
-                recv(name, c)
+        def R5(c=c, start=start, count=count, first=first, second=second, gathered=gathered, spread=spread):
+            recv(("second", c), pieces(count, 1, 2))
             if "momentum" not in waited:
                 waited.add("momentum")
                 momentum_load.wait()
@@ -241,64 +295,65 @@
             mine = gathered(at[first], at[second], every)
             send(("g_r", c), mine, mine, device(second, 1))
             send(("g_l", c), mine, mine, device(second, -1))
-            spread(c, first, gathered, 0)
-
-        def g6(c=c, first=first, second=second, gathered=gathered, spread=spread):
-            for name, step, rs in (("r", 1, low), ("l", -1, high)):
-                recv("g_" + name, c)
-                passed = gathered(at[first], shifted(second, -step), rs)
-                send(("h_" + name, c), passed, passed, device(second, step))
-            spread(c, first, gathered, 1)
-            spread(c, first, gathered, -1)
-
-        def g7(c=c, first=first, gathered=gathered, spread=spread):
-            recv("h_r", c)
-            recv("h_l", c)
-            spread(c, first, gathered, 2)
-
-        def g8(c=c, first=first, second=second, gathered=gathered):
-            for s in (0, 1, -1, 2):
-                for name, step, rs in (("r", 1, low), ("l", -1, high)):
-                    recv("G_" + name, s, c)
-                    passed = gathered(shifted(first, -step), shifted(second, s), rs)
-                    send(("H_" + name, s, c), passed, passed, device(first, step))
-
-        def g9(c=c):
-            for s in (0, 1, -1, 2):
-                recv("H_r", s, c)
-                recv("H_l", s, c)
-
-        for step in (e0, e1, e2, e3, r3, r4, r5, g6, g7, g8, g9):
+            spread(0)
+
+        def pass_on(name, step, rs, c=c, count=count, first=first, second=second, gathered=gathered, spread=spread):
+            recv(("g_" + name, c), pieces(count, 1, 1))
+            passed = gathered(at[first], shifted(second, -step), rs)
+            send(("h_" + name, c), passed, passed, device(second, step))
+            spread(-step)
+
+        def G6r(pass_on=pass_on):
+            pass_on("r", 1, low)
+
+        def G6l(pass_on=pass_on):
+            pass_on("l", -1, high)
+
+        def G7(c=c, count=count, spread=spread):
+            recv(("far", c), pieces(count, 1, 1))
+            spread(2)
+
+        def last_pass(s, name, step, rs, c=c, count=count, first=first, second=second, gathered=gathered):
+            recv(("G_" + name, s, c), pieces(count, 1, 1))
+            passed = gathered(shifted(first, -step), shifted(second, s), rs)
+            send(("H_" + name, s, c), passed, passed, device(first, step))
+
+        def G9(c=c, count=count):
+            recv(("last", c), pieces(count, 4, 1))
+
+        for step in (E2, E1r, E1l, E0, Sp, Swr, Swl, A2r, A2l, R3a, R3b, R3c, R4r, R4l, R5, G6r, G6l, G7, G9):
             steps[step.__name__, c] = step
+        for s in (0, 1, -1, 2):
+            steps["G8r", c, s] = functools.partial(last_pass, s, "r", 1, low)
+            steps["G8l", c, s] = functools.partial(last_pass, s, "l", -1, high)
 
     def norm_round(i, place, target):
         for step in (1, 2, 3):
-            send(("n", i, step), norm_ref.at[i, place], norm_ref.at[i, place], target(step))
+            send((f"n{i}", len(CHUNKS)), norm_ref.at[i, place], norm_ref.at[i, place], target(step))
 
     def norm_sum(i):
-        for step in (1, 2, 3):
-            recv("n", i, step)
+        recv((f"n{i}", len(CHUNKS)), norm_ref.at[0, pl.ds(0, 3)])
         return norm_ref[i, 0] + norm_ref[i, 1] + norm_ref[i, 2] + norm_ref[i, 3]
 
     other = z_lo * 2 + near
 
-    def n0():
+    def N0():
         norm_ref[0, at["x"]] = squares_ref[...]
         norm_round(0, at["x"], lambda step: device("x", step))
 
-    def n1():
+    def N1():
         norm_ref[1, at["z"]] = norm_sum(0)
         norm_round(1, at["z"], lambda step: device("z", step))
 
-    def n2():
+    def N2():
         norm_ref[2, y] = norm_sum(1)
         norm_round(2, y, lambda step: fsdp_device("y", step))
 
-    def n3():
+    def N3():
         norm_ref[3, other] = norm_sum(2)
         norm_round(3, other, lambda step: fsdp_device("other", step))
 
-    for step in (n0, n1, n2, n3):
+    for step in (N0, N1, N2, N3):
         steps[step.__name__, 0] = step
 
     for key in ORDER:
@@ -306,12 +361,34 @@
     total = jnp.sum(norm_sum(3), axis=(0, 1), keepdims=True)
     entries = rows * columns * 16
     rms_ref[...] = jnp.broadcast_to(jnp.sqrt(total / entries), rms_ref.shape)
-    for copy in copies.values():
-        copy.wait_send()
+    for c, (_, count, _) in enumerate(CHUNKS):
+        wide, high_, deep = SENT[count]
+        wait(send_sem.at[c], coded_ref.at[pl.ds(0, wide), pl.ds(0, high_), pl.ds(0, deep)])
+    wait(send_sem.at[len(CHUNKS)], norm_ref.at[pl.ds(0, 3)])
 
 
 second_of = {"x": "z", "z": "x"}
-COPIES = len(CHUNKS) * (4 + 2 + 2 + 4 + 8 + 8 + 4) + 12
+SPLIT = 1
+RECEIVES = len(CHUNKS) * 18 + 4
+GROUP = {
+    "w_r": "first", "w_l": "first", "s_r": "first", "s_l": "first",
+    "W_r": "second", "W_l": "second", "S_r": "second", "S_l": "second",
+    "h_r": "far", "h_l": "far", "H_r": "last", "H_l": "last",
+}
+SENT = {1: (10, 3, 1), 2: (5, 4, 3), 3: (10, 3, 3), 4: (10, 4, 3)}
+
+
+def write_out(params_ref, momentum_ref, rms_ref, params_hbm, momentum_hbm, rms_hbm, sem):
+    copies = [pltpu.make_async_copy(rms_ref, rms_hbm, sem.at[0])]
+    for src, dst in ((params_ref, params_hbm), (momentum_ref, momentum_hbm)):
+        step = src.shape[0] // SPLIT
+        for i in range(SPLIT):
+            part = pl.ds(i * step, step)
+            copies.append(pltpu.make_async_copy(src.at[part], dst.at[part], sem.at[len(copies)]))
+    for copy in copies:
+        copy.start()
+    for copy in copies:
+        copy.wait()
 
 
 def per_device(base, local, momentum):
@@ -326,7 +403,7 @@
         out_shape=(
             pltpu.VMEM((rows, columns), jnp.bfloat16),
             pltpu.VMEM((rows, piece), jnp.float32),
-            pltpu.VMEM((8, LANES), jnp.float32),
+            pltpu.VMEM((1, 1), jnp.float32),
         ),
         in_specs=[pl.BlockSpec(memory_space=pltpu.HBM)] * 3,
         out_specs=(vmem, vmem, vmem),
@@ -346,14 +423,28 @@
             pltpu.VMEM((8, LANES), jnp.float32),
             pltpu.VMEM((4, 4, 8, LANES), jnp.float32),
             pltpu.SemaphoreType.DMA((9,)),
-            pltpu.SemaphoreType.DMA((COPIES,)),
-            pltpu.SemaphoreType.DMA((COPIES,)),
+            pltpu.SemaphoreType.DMA((len(CHUNKS) + 1,)),
+            pltpu.SemaphoreType.DMA((RECEIVES,)),
         ],
         compiler_params=pltpu.CompilerParams(
-            collective_id=0, has_side_effects=True, vmem_limit_bytes=40 * 2**20
+            collective_id=0, has_side_effects=True, vmem_limit_bytes=24 * 2**20
         ),
         name="outer_step",
     )(*(pltpu.with_memory_space_constraint(a, pltpu.HBM) for a in (base, local, momentum)))
+    hbm = pl.BlockSpec(memory_space=pltpu.HBM)
+    new_params, new_momentum, rms = pl.pallas_call(
+        write_out,
+        out_shape=(
+            pltpu.HBM((rows, columns), jnp.bfloat16),
+            pltpu.HBM((rows, piece), jnp.float32),
+            pltpu.HBM((1, 1), jnp.float32),
+        ),
+        in_specs=[vmem] * 3,
+        out_specs=(hbm,) * 3,
+        scratch_shapes=[pltpu.SemaphoreType.DMA((2 * SPLIT + 1,))],
+        compiler_params=pltpu.CompilerParams(vmem_limit_bytes=2**20),
+        name="write_out",
+    )(*(pltpu.with_memory_space_constraint(a, pltpu.VMEM) for a in (new_params, new_momentum, rms)))
     return (new_params, new_momentum, rms[0, 0])
 
 

time: 83.7 us -> 71.8 us (0.86)
  Pallas kernels: 79.2 us -> 70.6 us
  local copies, waits for them, and re-layouts: 3.12 us -> 0 us
    pallas_call x1, Pallas kernels: 79.2 us -> 68 us  [per_device(): pl.pallas_call(kernel, out_shape=(pltpu.VMEM((rows, columns), jnp.bfloat1...]
    pallas_call x0 -> x1, Pallas kernels: none -> 2.64 us  [per_device(): pl.pallas_call(write_out, out_shape=(pltpu.HBM((rows, columns), jnp.bfloa...]
    unnamed x2 -> x0, local copies, waits for them, and re-layouts: 2.6 us -> none
where the time goes in v2:
time: 71.8 us; the launch traced here: 71.3 us
  Pallas kernels  70.6 us (98%)
    pallas_call x1, Pallas kernels, per_device(): pl.pallas_call(kernel, out_shape=(pltpu.VMEM((rows, columns), jnp.bfloat1...  68 us
    pallas_call x1, Pallas kernels, per_device(): pl.pallas_call(write_out, out_shape=(pltpu.HBM((rows, columns), jnp.bfloa...  2.64 us

profile of v2, /device:TPU:1, one launch (start us, length us, event | category | flops | bytes accessed | tf_op | source)
XLA Modules:
  0.0 71.3 jit_solution(17057834079926381244)
XLA Ops:
  0.6 68.0 %outer_step.1 = (bf16[64,28672]{1,0:T(8,128)(2,1)S(1)}, f32[64,1792]{1,0:T(8,128)S(1)}, f32[1,1]{1,0:T(1,128)}) custom-call(bf16[64,28672]{1,0:T(8,128)(2,1)} %base_hbm.1, bf16[1,64,28672]{2,1,0:T(8,128)(2,1)} %local_hbm.1, f32[64,1792]{1,0:T(8,128)} %momentum_hbm.1), custom_call_target="tpu_custom_call" | custom-call | tf_op jit(solution)/shard_map/outer_step/pallas_call | solution.py:401
  68.6 2.6 %write_out.1 = (bf16[64,28672]{1,0:T(8,128)(2,1)}, f32[64,1792]{1,0:T(8,128)}, f32[1,1]{1,0:T(1,128)}) custom-call(bf16[64,28672]{1,0:T(8,128)(2,1)S(1)} %get-tuple-element.9.params_ref, f32[64,1792]{1,0:T(8,128)S(1)} %get-tuple-element.10.momentum_ref, f32[1,1]{1,0:T(1,128)} %get-tuple-element.11.rms_ref), custom_call_target="tpu_custom_call" | custom-call | tf_op jit(solution)/shard_map/write_out/pallas_call | solution.py:435

commit v3 on v2

--- a/solution.py
+++ b/solution.py
@@ -25,29 +25,29 @@
     (10, 1, "x"),
 )
 ORDER = (
-    ("E2", 2), ("Sp", 2), ("E2", 5), ("E2", 1), ("Sp", 5), ("E2", 0), ("Sp", 0), ("Sp", 1), ("E1l", 2), ("E1r", 0), ("Swr", 0), ("Swl", 2), ("E2", 3),
-    ("E1l", 5), ("E1l", 0), ("E1r", 2), ("Swl", 5), ("Swl", 0), ("Sp", 3), ("Swr", 2), ("A2r", 2), ("E1r", 5), ("E1l", 1), ("E1l", 8), ("A2l", 2),
-    ("A2r", 0), ("Swr", 5), ("E1r", 1), ("A2l", 0), ("Swl", 8), ("A2r", 5), ("A2l", 5), ("E2", 7), ("A2l", 1), ("E2", 4), ("E2", 8), ("Sp", 8),
-    ("E1r", 8), ("A2r", 1), ("Sp", 4), ("E1l", 4), ("E2", 6), ("Swr", 8), ("E0", 2), ("R3a", 2), ("E1l", 3), ("Swl", 1), ("Sp", 6), ("Swr", 1),
-    ("E0", 3), ("E0", 0), ("E1l", 6), ("Sp", 7), ("R3a", 0), ("E1r", 4), ("A2r", 8), ("R3b", 2), ("A2l", 8), ("E0", 5), ("R3b", 0), ("Swl", 4),
-    ("R3c", 2), ("Swr", 4), ("E1r", 6), ("R4r", 2), ("R4l", 2), ("A2l", 4), ("A2l", 3), ("E1r", 3), ("Swr", 3), ("E1r", 7), ("Swl", 6), ("A2r", 4),
-    ("E0", 4), ("A2l", 6), ("R4r", 0), ("R4l", 0), ("Swr", 6), ("Swl", 3), ("A2r", 6), ("A2r", 3), ("A2r", 7), ("Swr", 7), ("E1l", 7), ("E0", 8),
-    ("R3a", 8), ("Swl", 7), ("R3b", 8), ("R3c", 0), ("A2l", 7), ("R5", 2), ("R3a", 5), ("E0", 6), ("R3a", 4), ("R5", 0), ("R3b", 4), ("R3a", 3),
-    ("E0", 7), ("R3c", 3), ("R3a", 6), ("R4l", 8), ("R3c", 4), ("R4r", 8), ("R3c", 8), ("E0", 1), ("G6r", 2), ("G6l", 2), ("R3b", 6), ("R4l", 4),
-    ("R4r", 4), ("R3a", 7), ("R3a", 1), ("R3b", 5), ("R4r", 5), ("R4l", 5), ("G6l", 0), ("G6r", 0), ("R3c", 6), ("R3c", 5), ("R4r", 6), ("R4l", 6),
-    ("R3b", 3), ("R5", 8), ("R3b", 7), ("G8l", 2, 0), ("R3c", 7), ("R4r", 3), ("R3b", 1), ("G8l", 2, -1), ("R5", 5), ("G7", 2), ("R4r", 7),
-    ("R4l", 7), ("R4l", 3), ("R4l", 1), ("G8r", 2, 1), ("R4r", 1), ("G8l", 0, 1), ("R5", 4), ("G8r", 0, 0), ("G6r", 8), ("R3c", 1), ("G6l", 8),
-    ("R5", 6), ("R5", 3), ("G7", 0), ("R5", 7), ("R5", 1), ("N0", 0), ("G8r", 0, -1), ("G8l", 0, 0), ("G8l", 4, 0), ("G8r", 0, 1), ("G6l", 4),
-    ("G6r", 4), ("G8r", 8, 1), ("G8l", 2, 1), ("G6l", 3), ("G6r", 3), ("G8l", 0, -1), ("G6r", 6), ("G7", 8), ("G8l", 0, 2), ("G8r", 2, 0), ("G6r", 1),
-    ("G6l", 1), ("G6r", 7), ("G8r", 2, -1), ("G8r", 6, 0), ("G6r", 5), ("G6l", 7), ("G8r", 4, -1), ("G8r", 8, -1), ("G6l", 5), ("N1", 0), ("G7", 4),
-    ("G6l", 6), ("G8l", 2, 2), ("G8l", 4, -1), ("G8r", 4, 0), ("G8l", 3, 0), ("G7", 1), ("G8r", 7, 0), ("G7", 3), ("G8r", 4, 1), ("G8l", 6, 0),
-    ("G8l", 6, -1), ("G8r", 0, 2), ("G8r", 8, 2), ("G8l", 4, 1), ("G7", 5), ("G8l", 7, 0), ("G8r", 3, 0), ("G8l", 3, -1), ("G7", 7), ("G8r", 3, -1),
-    ("G8l", 5, -1), ("N2", 0), ("G8l", 8, 1), ("G8l", 1, -1), ("G8r", 3, 1), ("G8l", 8, 0), ("G8r", 5, -1), ("G8l", 1, 1), ("G8r", 6, -1), ("G7", 6),
-    ("G8r", 1, 0), ("G8l", 8, 2), ("G8r", 7, 1), ("G8r", 1, -1), ("G8r", 5, 0), ("G8l", 5, 1), ("G8l", 3, 1), ("G8r", 4, 2), ("G8r", 1, 2),
-    ("G8l", 7, -1), ("G8r", 1, 1), ("G8r", 7, -1), ("G8r", 2, 2), ("N3", 0), ("G8r", 3, 2), ("G8l", 1, 0), ("G8l", 4, 2), ("G8l", 6, 1),
-    ("G8l", 1, 2), ("G8l", 3, 2), ("G8r", 6, 1), ("G8r", 5, 2), ("G8r", 8, 0), ("G8l", 8, -1), ("G8r", 7, 2), ("G8l", 7, 2), ("G8r", 5, 1),
-    ("G8l", 5, 2), ("G8l", 5, 0), ("G8l", 7, 1), ("G8r", 6, 2), ("G8l", 6, 2), ("G9", 0), ("G9", 2), ("G9", 4), ("G9", 8), ("G9", 1), ("G9", 7),
-    ("G9", 3), ("G9", 6), ("G9", 5),
+    ("E2", 0), ("Sp", 0), ("E2", 1), ("E2", 6), ("E2", 4), ("Sp", 1), ("Sp", 4), ("Sp", 6), ("E1l", 4), ("E1r", 4), ("E2", 5), ("Swl", 4), ("Swr", 4),
+    ("Sp", 5), ("E2", 3), ("E2", 2), ("E1r", 3), ("E2", 8), ("Sp", 2), ("Sp", 3), ("E1l", 1), ("E1r", 1), ("Swl", 1), ("Swr", 3), ("E0", 4),
+    ("Swr", 1), ("E1l", 3), ("A2l", 4), ("A2r", 4), ("A2l", 1), ("E1l", 5), ("E1r", 6), ("E1l", 6), ("A2l", 6), ("Swr", 6), ("Swl", 5), ("A2r", 6),
+    ("Swl", 3), ("Swl", 6), ("A2r", 1), ("E1r", 0), ("Swr", 0), ("E1r", 5), ("Swr", 5), ("A2r", 0), ("E0", 6), ("E1l", 0), ("E1l", 2), ("Swl", 0),
+    ("R3a", 4), ("A2l", 0), ("R3b", 4), ("A2r", 3), ("Sp", 8), ("Swl", 2), ("A2l", 3), ("E1r", 2), ("E1r", 7), ("E0", 3), ("Swr", 2), ("R3c", 4),
+    ("A2l", 2), ("E1r", 8), ("R3a", 6), ("A2r", 5), ("E0", 1), ("A2l", 5), ("E2", 7), ("A2r", 2), ("R4l", 4), ("E1l", 8), ("R4r", 4), ("E0", 0),
+    ("R3a", 0), ("Sp", 7), ("Swl", 8), ("R3b", 6), ("R3b", 0), ("A2r", 8), ("R3c", 0), ("E1l", 7), ("E0", 2), ("Swr", 8), ("A2l", 8), ("Swr", 7),
+    ("R4l", 6), ("E0", 8), ("R4r", 6), ("E0", 5), ("Swl", 7), ("R3a", 2), ("R5", 4), ("R4l", 0), ("A2l", 7), ("A2r", 7), ("R4r", 0), ("R3b", 2),
+    ("R3a", 5), ("E0", 7), ("R3c", 6), ("R3a", 1), ("R3a", 3), ("R3a", 8), ("R5", 6), ("G8r", 4, 0), ("R4r", 2), ("R3c", 2), ("R3b", 3), ("R4l", 2),
+    ("R3c", 8), ("R3b", 1), ("R3c", 3), ("R3b", 5), ("R3b", 8), ("R3a", 7), ("G6r", 4), ("G6l", 4), ("R4r", 3), ("R5", 0), ("G8l", 6, 0), ("R4l", 5),
+    ("R4r", 8), ("R4r", 5), ("G8r", 6, 0), ("R4l", 8), ("G8l", 4, 0), ("R3c", 7), ("R3b", 7), ("R4l", 1), ("R4r", 1), ("R4l", 3), ("R5", 2),
+    ("G8r", 4, -1), ("R4l", 7), ("G6l", 6), ("R4r", 7), ("G8l", 4, -1), ("G7", 4), ("G6r", 6), ("G8r", 0, 0), ("R5", 8), ("R5", 3), ("G6l", 0),
+    ("G6r", 0), ("G8l", 6, 1), ("R3c", 1), ("R5", 1), ("R3c", 5), ("G8r", 6, 1), ("R5", 7), ("R5", 5), ("N0", 0), ("G6r", 2), ("G8l", 8, 0),
+    ("G6r", 8), ("G6l", 3), ("G8r", 4, 2), ("G6l", 2), ("G6l", 8), ("G6r", 1), ("G7", 0), ("G8r", 8, 0), ("G8l", 7, 0), ("G6l", 1), ("G6r", 3),
+    ("G8r", 0, 1), ("G6l", 7), ("N1", 0), ("G6r", 7), ("G6r", 5), ("G6l", 5), ("G8l", 2, 0), ("G7", 6), ("G8r", 7, 0), ("G8l", 6, -1), ("G8r", 2, 0),
+    ("G8r", 2, 1), ("G8l", 0, -1), ("G8l", 4, 1), ("G8l", 8, 1), ("G7", 2), ("G7", 8), ("G8l", 0, 2), ("G8r", 8, -1), ("G7", 1), ("G7", 3),
+    ("G8l", 1, -1), ("G8r", 0, -1), ("G8r", 2, -1), ("G8r", 0, 2), ("G8l", 0, 1), ("G8r", 7, 1), ("G8l", 2, -1), ("G8r", 3, -1), ("G7", 5),
+    ("G8r", 1, 0), ("G8l", 3, 0), ("G8l", 1, 1), ("G8r", 3, 1), ("G7", 7), ("G8r", 8, 1), ("G8r", 4, 1), ("G8l", 3, 1), ("G8r", 3, 0), ("G8l", 4, 2),
+    ("G8l", 2, 1), ("G8r", 1, 1), ("G8l", 1, 0), ("N2", 0), ("G8l", 3, -1), ("G8l", 7, -1), ("G8r", 1, -1), ("G8l", 0, 0), ("G8r", 6, -1),
+    ("G8r", 6, 2), ("G8l", 8, -1), ("G8l", 1, 2), ("G8l", 5, 1), ("G8r", 1, 2), ("G8r", 7, -1), ("G8r", 5, -1), ("G8r", 5, 0), ("G8l", 5, 0),
+    ("G8l", 6, 2), ("G8l", 3, 2), ("G8l", 2, 2), ("G8r", 3, 2), ("G8l", 8, 2), ("G8r", 2, 2), ("G8l", 5, -1), ("G8r", 5, 1), ("G8r", 8, 2),
+    ("G8l", 5, 2), ("G8r", 5, 2), ("G8l", 7, 1), ("G8r", 7, 2), ("G8l", 7, 2), ("N3", 0), ("G9", 0), ("G9", 1), ("G9", 4), ("G9", 6), ("G9", 8),
+    ("G9", 2), ("G9", 3), ("G9", 7), ("G9", 5),
 )
 
 
@@ -55,7 +55,7 @@
     base_hbm, local_hbm, momentum_hbm, params_ref, new_momentum_ref, rms_ref,
     base_ref, local_ref, momentum_ref, coded_ref,
     full_l, full_r, half_l, half_r, last_l, last_r, part_l, part_r,
-    squares_ref, norm_ref, load_sem, send_sem, recv_sem,
+    squares_ref, norm_ref, early_ref, load_sem, send_sem, recv_sem,
 ):
     rows, columns = base_ref.shape
     half = rows // 2
@@ -82,6 +82,20 @@
             return (replica, z_lo * 8 + (y + step) % 4 * 2 + near)
         other = (z_lo * 2 + near + step) % 4
         return (replica, other // 2 * 8 + y * 2 + other % 2)
+
+    barrier = pltpu.get_barrier_semaphore()
+    peers = [device(axis, step) for axis in ("x", "z") for step in (1, 2, 3)]
+    peers += [fsdp_device(axis, step) for axis in ("y", "other") for step in (1, 2, 3)]
+    for peer in peers:
+        pl.semaphore_signal(barrier, inc=1, device_id=peer, device_id_type=MESH)
+
+    for c, (start, count, first) in enumerate(CHUNKS[:EARLY]):
+        for s in range(SIDE):
+            x, z = (shifted("x", 2), s) if first == "x" else (s, shifted("z", 2))
+            cols = pl.ds(pl.multiple_of((x * SIDE + z) * piece + start * LANES, LANES), count * LANES)
+            for i, src in enumerate((base_hbm.at[:, cols], local_hbm.at[0, :, cols])):
+                dst = early_ref.at[c, i, s, :, pl.ds(0, count * LANES)]
+                pltpu.make_async_copy(src, dst, load_sem.at[9 + c]).start()
 
     group = SIDE * piece
     loads = {}
@@ -95,15 +109,9 @@
             copy.start()
     momentum_load = pltpu.make_async_copy(momentum_hbm, momentum_ref, load_sem.at[8])
     momentum_load.start()
-    squares_ref[...] = jnp.zeros_like(squares_ref)
-
-    barrier = pltpu.get_barrier_semaphore()
-    peers = [device(axis, step) for axis in ("x", "z") for step in (1, 2, 3)]
-    peers += [fsdp_device(axis, step) for axis in ("y", "other") for step in (1, 2, 3)]
-    for peer in peers:
-        pl.semaphore_signal(barrier, inc=1, device_id=peer, device_id_type=MESH)
     entered = []
     waited = set()
+    squares_ref[...] = jnp.zeros_like(squares_ref)
 
     def loaded(step):
         if step not in waited:
@@ -117,7 +125,11 @@
         if not entered:
             entered.append(True)
             pl.semaphore_wait(barrier, len(peers))
-        together = (GROUP[key[0]], key[-1]) if key[0] in GROUP else key
+        together = key
+        if key[0] in GROUP:
+            together = (GROUP[key[0]], key[-1])
+        elif key[0] in ("G_r", "G_l"):
+            together = ("G", *key[1:])
         i = groups.setdefault(together, len(groups))
         pltpu.make_async_remote_copy(
             src_ref=src, dst_ref=dst, send_sem=send_sem.at[key[-1]], recv_sem=recv_sem.at[i],
@@ -128,10 +140,12 @@
         pltpu.make_async_copy(sized, sized, sem).wait()
 
     def recv(key, sized):
-        wait(recv_sem.at[groups[key]], sized)
-
-    def pieces(count, x, z, rs=slice(None)):
-        return coded_ref.at[pl.ds(0, count), pl.ds(0, x), pl.ds(0, z), rs]
+        if key not in waited:
+            waited.add(key)
+            wait(recv_sem.at[groups[key]], sized)
+
+    def pieces(count, x, z):
+        return coded_ref.at[pl.ds(0, count), pl.ds(0, x), pl.ds(0, z)]
 
     low, high, every = pl.ds(0, half), pl.ds(half, half), pl.ds(0, rows)
 
@@ -140,7 +154,10 @@
 
     def code_block(block, x, z):
         cols = pl.ds(column(x, z, block), LANES)
-        delta = base_ref[:, cols].astype(jnp.float32) - local_ref[:, cols].astype(jnp.float32)
+        code_values(block, x, z, base_ref[:, cols], local_ref[:, cols])
+
+    def code_values(block, x, z, base, local):
+        delta = base.astype(jnp.float32) - local.astype(jnp.float32)
         largest = jnp.max(jnp.abs(delta), axis=1, keepdims=True)
         scale = ((largest + 1e-06) * (1.0 / 448.0)).astype(jnp.bfloat16).astype(jnp.float32)
         coded = (delta / scale).astype(jnp.bfloat16).astype(jnp.float32)
@@ -190,8 +207,17 @@
             over(start, count, lambda block, s: code_block(block, *xz(f, s)))
 
 
-        def E2(code=code):
-            code(2)
+        def E2(c=c, start=start, count=count, first=first, code=code, xz=xz):
+            if c >= EARLY:
+                code(2)
+                return
+            wait(load_sem.at[9 + c], early_ref.at[c, :, :, :, pl.ds(0, count * LANES)])
+            f = shifted(first, 2)
+
+            def early(block, s):
+                cols = pl.ds(pl.multiple_of((block - start) * LANES, LANES), LANES)
+                code_values(block, *xz(f, s), early_ref[c, 0, s, :, cols], early_ref[c, 1, s, :, cols])
+            over(start, count, early)
 
         def E1r(code=code):
             code(1)
@@ -215,7 +241,7 @@
 
         def join(name, step, rs, got, into, c=c, ks=ks, start=start, count=count, first=first, row_of=row_of, xz=xz):
             f = shifted(first, step)
-            recv(("p_" + name, c), pieces(count, 4, 1, low))
+            recv(("p", c), pieces(count, 4, 1))
 
             def add(block, s):
                 index = (block, *xz(f, s), rs)
@@ -255,7 +281,7 @@
         def last_join(name, step, rs, got, into, c=c, ks=ks, start=start, count=count, first=first, second=second,
                       piece_of=piece_of, xz=xz):
             s = shifted(second, step)
-            recv(("P_" + name, c), pieces(count, 1, 1, low))
+            recv(("P", c), pieces(count, 1, 1))
 
             def add(block):
                 index = (block, *xz(at[first], s), rs)
@@ -298,7 +324,7 @@
             spread(0)
 
         def pass_on(name, step, rs, c=c, count=count, first=first, second=second, gathered=gathered, spread=spread):
-            recv(("g_" + name, c), pieces(count, 1, 1))
+            recv(("g", c), pieces(count, 1, 2))
             passed = gathered(at[first], shifted(second, -step), rs)
             send(("h_" + name, c), passed, passed, device(second, step))
             spread(-step)
@@ -314,7 +340,7 @@
             spread(2)
 
         def last_pass(s, name, step, rs, c=c, count=count, first=first, second=second, gathered=gathered):
-            recv(("G_" + name, s, c), pieces(count, 1, 1))
+            recv(("G", s, c), pieces(count, 1, 2))
             passed = gathered(shifted(first, -step), shifted(second, s), rs)
             send(("H_" + name, s, c), passed, passed, device(first, step))
 
@@ -369,8 +395,10 @@
 
 second_of = {"x": "z", "z": "x"}
 SPLIT = 1
-RECEIVES = len(CHUNKS) * 18 + 4
+EARLY = 2
+RECEIVES = len(CHUNKS) * 11 + 4
 GROUP = {
+    "p_r": "p", "p_l": "p", "P_r": "P", "P_l": "P", "g_r": "g", "g_l": "g",
     "w_r": "first", "w_l": "first", "s_r": "first", "s_l": "first",
     "W_r": "second", "W_l": "second", "S_r": "second", "S_l": "second",
     "h_r": "far", "h_l": "far", "H_r": "last", "H_l": "last",
@@ -422,7 +450,8 @@
             bf16((number, half, LANES)),
             pltpu.VMEM((8, LANES), jnp.float32),
             pltpu.VMEM((4, 4, 8, LANES), jnp.float32),
-            pltpu.SemaphoreType.DMA((9,)),
+            bf16((EARLY, 2, SIDE, rows, max(c[1] for c in CHUNKS[:EARLY]) * LANES)),
+            pltpu.SemaphoreType.DMA((9 + EARLY,)),
             pltpu.SemaphoreType.DMA((len(CHUNKS) + 1,)),
             pltpu.SemaphoreType.DMA((RECEIVES,)),
         ],

time: 71.8 us -> 70.3 us (0.979)
  Pallas kernels: 70.6 us -> 69.5 us
    pallas_call x1, Pallas kernels: 68 us -> 66.9 us  [per_device(): pl.pallas_call(kernel, out_shape=(pltpu.VMEM((rows, columns), jnp.bfloat1...]
where the time goes in v3:
time: 70.3 us; the launch traced here: 70.2 us
  Pallas kernels  69.5 us (99%)
    pallas_call x1, Pallas kernels, per_device(): pl.pallas_call(kernel, out_shape=(pltpu.VMEM((rows, columns), jnp.bfloat1...  66.9 us
    pallas_call x1, Pallas kernels, per_device(): pl.pallas_call(write_out, out_shape=(pltpu.HBM((rows, columns), jnp.bfloa...  2.64 us

profile of v3, /device:TPU:1, one launch (start us, length us, event | category | flops | bytes accessed | tf_op | source)
XLA Modules:
  0.0 70.2 jit_solution(11355590207530938219)
XLA Ops:
  0.6 66.9 %outer_step.1 = (bf16[64,28672]{1,0:T(8,128)(2,1)S(1)}, f32[64,1792]{1,0:T(8,128)S(1)}, f32[1,1]{1,0:T(1,128)}) custom-call(bf16[64,28672]{1,0:T(8,128)(2,1)} %base_hbm.1, bf16[1,64,28672]{2,1,0:T(8,128)(2,1)} %local_hbm.1, f32[64,1792]{1,0:T(8,128)} %momentum_hbm.1), custom_call_target="tpu_custom_call" | custom-call | tf_op jit(solution)/shard_map/outer_step/pallas_call | solution.py:429
  67.5 2.6 %write_out.1 = (bf16[64,28672]{1,0:T(8,128)(2,1)}, f32[64,1792]{1,0:T(8,128)}, f32[1,1]{1,0:T(1,128)}) custom-call(bf16[64,28672]{1,0:T(8,128)(2,1)S(1)} %get-tuple-element.9.params_ref, f32[64,1792]{1,0:T(8,128)S(1)} %get-tuple-element.10.momentum_ref, f32[1,1]{1,0:T(1,128)} %get-tuple-element.11.rms_ref), custom_call_target="tpu_custom_call" | custom-call | tf_op jit(solution)/shard_map/write_out/pallas_call | solution.py:464

commit v4 on v3

--- a/solution.py
+++ b/solution.py
@@ -121,6 +121,11 @@
 
     groups = {}
 
+    def slot(key):
+        if key[:2] == ("G", 0):
+            return ("p", key[-1])
+        return (REUSED.get(key[0], key[0]), *key[1:])
+
     def send(key, src, dst, target):
         if not entered:
             entered.append(True)
@@ -130,7 +135,7 @@
             together = (GROUP[key[0]], key[-1])
         elif key[0] in ("G_r", "G_l"):
             together = ("G", *key[1:])
-        i = groups.setdefault(together, len(groups))
+        i = groups.setdefault(slot(together), len(groups))
         pltpu.make_async_remote_copy(
             src_ref=src, dst_ref=dst, send_sem=send_sem.at[key[-1]], recv_sem=recv_sem.at[i],
             device_id=target, device_id_type=MESH,
@@ -142,7 +147,7 @@
     def recv(key, sized):
         if key not in waited:
             waited.add(key)
-            wait(recv_sem.at[groups[key]], sized)
+            wait(recv_sem.at[groups[slot(key)]], sized)
 
     def pieces(count, x, z):
         return coded_ref.at[pl.ds(0, count), pl.ds(0, x), pl.ds(0, z)]
@@ -396,7 +401,8 @@
 second_of = {"x": "z", "z": "x"}
 SPLIT = 1
 EARLY = 2
-RECEIVES = len(CHUNKS) * 11 + 4
+RECEIVES = len(CHUNKS) * 7 + 4
+REUSED = {"g": "P", "last": "first", "far": "second"}
 GROUP = {
     "p_r": "p", "p_l": "p", "P_r": "P", "P_l": "P", "g_r": "g", "g_l": "g",
     "w_r": "first", "w_l": "first", "s_r": "first", "s_l": "first",

time: 70.3 us -> 70 us (level)
  no operation moved by 1% of the time
where the time goes in v4:
time: 70 us; the launch traced here: 69.9 us
  Pallas kernels  69.2 us (99%)
    pallas_call x1, Pallas kernels, per_device(): pl.pallas_call(kernel, out_shape=(pltpu.VMEM((rows, columns), jnp.bfloat1...  66.6 us
    pallas_call x1, Pallas kernels, per_device(): pl.pallas_call(write_out, out_shape=(pltpu.HBM((rows, columns), jnp.bfloa...  2.64 us

profile of v4, /device:TPU:1, one launch (start us, length us, event | category | flops | bytes accessed | tf_op | source)
XLA Modules:
  0.0 69.9 jit_solution(7969754849515504253)
XLA Ops:
  0.6 66.6 %outer_step.1 = (bf16[64,28672]{1,0:T(8,128)(2,1)S(1)}, f32[64,1792]{1,0:T(8,128)S(1)}, f32[1,1]{1,0:T(1,128)}) custom-call(bf16[64,28672]{1,0:T(8,128)(2,1)} %base_hbm.1, bf16[1,64,28672]{2,1,0:T(8,128)(2,1)} %local_hbm.1, f32[64,1792]{1,0:T(8,128)} %momentum_hbm.1), custom_call_target="tpu_custom_call" | custom-call | tf_op jit(solution)/shard_map/outer_step/pallas_call | solution.py:435
  67.2 2.6 %write_out.1 = (bf16[64,28672]{1,0:T(8,128)(2,1)}, f32[64,1792]{1,0:T(8,128)}, f32[1,1]{1,0:T(1,128)}) custom-call(bf16[64,28672]{1,0:T(8,128)(2,1)S(1)} %get-tuple-element.9.params_ref, f32[64,1792]{1,0:T(8,128)S(1)} %get-tuple-element.10.momentum_ref, f32[1,1]{1,0:T(1,128)} %get-tuple-element.11.rms_ref), custom_call_target="tpu_custom_call" | custom-call | tf_op jit(solution)/shard_map/write_out/pallas_call | solution.py:470

commit v5 on v4

--- a/solution.py
+++ b/solution.py
@@ -165,7 +165,7 @@
         delta = base.astype(jnp.float32) - local.astype(jnp.float32)
         largest = jnp.max(jnp.abs(delta), axis=1, keepdims=True)
         scale = ((largest + 1e-06) * (1.0 / 448.0)).astype(jnp.bfloat16).astype(jnp.float32)
-        coded = (delta / scale).astype(jnp.bfloat16).astype(jnp.float32)
+        coded = (delta * (1.0 / scale)).astype(jnp.bfloat16).astype(jnp.float32)
         coded_ref[block, x, z] = (coded * scale).astype(jnp.bfloat16)
 
     def over(start, count, body, unroll=2):
@@ -251,7 +251,7 @@
             def add(block, s):
                 index = (block, *xz(f, s), rs)
                 coded_ref[index] = (f32(coded_ref[index]) + f32(got[block, s])).astype(jnp.bfloat16)
-            over(start, count, add)
+            over(start, count, add, unroll=4)
             send(("s_" + name, c), row_of(f, rs), into.at[ks, :, rs], device(first, step))
 
         def A2r(join=join):
@@ -387,11 +387,13 @@
     for step in (N0, N1, N2, N3):
         steps[step.__name__, 0] = step
 
-    for key in ORDER:
+    for key in ORDER[:-len(CHUNKS)]:
         steps[key]()
     total = jnp.sum(norm_sum(3), axis=(0, 1), keepdims=True)
     entries = rows * columns * 16
     rms_ref[...] = jnp.broadcast_to(jnp.sqrt(total / entries), rms_ref.shape)
+    for key in ORDER[-len(CHUNKS):]:
+        steps[key]()
     for c, (_, count, _) in enumerate(CHUNKS):
         wide, high_, deep = SENT[count]
         wait(send_sem.at[c], coded_ref.at[pl.ds(0, wide), pl.ds(0, high_), pl.ds(0, deep)])

time: 70 us -> 69.4 us (level)
  no operation moved by 1% of the time
where the time goes in v5:
time: 69.4 us
  Pallas kernels  68.7 us (99%)
    pallas_call x1, Pallas kernels, per_device(): pl.pallas_call(kernel, out_shape=(pltpu.VMEM((rows, columns), jnp.bfloat1...  66.1 us
    pallas_call x1, Pallas kernels, per_device(): pl.pallas_call(write_out, out_shape=(pltpu.HBM((rows, columns), jnp.bfloa...  2.64 us

profile of v5, /device:TPU:1, one launch (start us, length us, event | category | flops | bytes accessed | tf_op | source)
XLA Modules:
  0.0 69.4 jit_solution(3599690676968362761)
XLA Ops:
  0.6 66.1 %outer_step.1 = (bf16[64,28672]{1,0:T(8,128)(2,1)S(1)}, f32[64,1792]{1,0:T(8,128)S(1)}, f32[1,1]{1,0:T(1,128)}) custom-call(bf16[64,28672]{1,0:T(8,128)(2,1)} %base_hbm.1, bf16[1,64,28672]{2,1,0:T(8,128)(2,1)} %local_hbm.1, f32[64,1792]{1,0:T(8,128)} %momentum_hbm.1), custom_call_target="tpu_custom_call" | custom-call | tf_op jit(solution)/shard_map/outer_step/pallas_call | solution.py:437
  66.7 2.6 %write_out.1 = (bf16[64,28672]{1,0:T(8,128)(2,1)}, f32[64,1792]{1,0:T(8,128)}, f32[1,1]{1,0:T(1,128)}) custom-call(bf16[64,28672]{1,0:T(8,128)(2,1)S(1)} %get-tuple-element.9.params_ref, f32[64,1792]{1,0:T(8,128)S(1)} %get-tuple-element.10.momentum_ref, f32[1,1]{1,0:T(1,128)} %get-tuple-element.11.rms_ref), custom_call_target="tpu_custom_call" | custom-call | tf_op jit(solution)/shard_map/write_out/pallas_call | solution.py:472

commit v6 on v5

--- a/solution.py
+++ b/solution.py
@@ -222,7 +222,7 @@
             def early(block, s):
                 cols = pl.ds(pl.multiple_of((block - start) * LANES, LANES), LANES)
                 code_values(block, *xz(f, s), early_ref[c, 0, s, :, cols], early_ref[c, 1, s, :, cols])
-            over(start, count, early)
+            over(start, count, early, unroll=4)
 
         def E1r(code=code):
             code(1)

time: 69.4 us -> 69.6 us (level)
  no operation moved by 1% of the time
where the time goes in v6:
time: 69.6 us; the launch traced here: 69.5 us
  Pallas kernels  68.9 us (99%)
    pallas_call x1, Pallas kernels, per_device(): pl.pallas_call(kernel, out_shape=(pltpu.VMEM((rows, columns), jnp.bfloat1...  66.2 us
    pallas_call x1, Pallas kernels, per_device(): pl.pallas_call(write_out, out_shape=(pltpu.HBM((rows, columns), jnp.bfloa...  2.64 us

profile of v6, /device:TPU:1, one launch (start us, length us, event | category | flops | bytes accessed | tf_op | source)
XLA Modules:
  0.0 69.5 jit_solution(13439301008904538057)
XLA Ops:
  0.6 66.2 %outer_step.1 = (bf16[64,28672]{1,0:T(8,128)(2,1)S(1)}, f32[64,1792]{1,0:T(8,128)S(1)}, f32[1,1]{1,0:T(1,128)}) custom-call(bf16[64,28672]{1,0:T(8,128)(2,1)} %base_hbm.1, bf16[1,64,28672]{2,1,0:T(8,128)(2,1)} %local_hbm.1, f32[64,1792]{1,0:T(8,128)} %momentum_hbm.1), custom_call_target="tpu_custom_call" | custom-call | tf_op jit(solution)/shard_map/outer_step/pallas_call | solution.py:437
  66.9 2.6 %write_out.1 = (bf16[64,28672]{1,0:T(8,128)(2,1)}, f32[64,1792]{1,0:T(8,128)}, f32[1,1]{1,0:T(1,128)}) custom-call(bf16[64,28672]{1,0:T(8,128)(2,1)S(1)} %get-tuple-element.9.params_ref, f32[64,1792]{1,0:T(8,128)S(1)} %get-tuple-element.10.momentum_ref, f32[1,1]{1,0:T(1,128)} %get-tuple-element.11.rms_ref), custom_call_target="tpu_custom_call" | custom-call | tf_op jit(solution)/shard_map/write_out/pallas_call | solution.py:472
